TPU v7x, 256 devices: a whole 4x4x8 slice. The times are simulated.
256 devices in a mesh: orb: 4 (over z_hi), grid: 64 (over y, x, z_lo, core).
Axes of the slice: x: 4, y: 4, z: 8 (z_hi: 4, z_lo: 2; z = z_hi * 2 + z_lo), core: 2. Of those that a mesh axis runs over, the one named last changes fastest.
Arguments:
- orbitals: bfloat16 [512, 884736], P(('orb', 'grid')), may hold values from -6 to 6
- potential: float32 [884736], replicated, may hold values from -1 to 1
- subspace: bfloat16 [512, 512], P(('orb', 'grid')), may hold values from -0.25 to 0.25
Outputs:
- rotated: bfloat16 [512, 884736], P(None, ('orb', 'grid'))
All inputs are finite; a program needn't handle non-finite values.
Results may differ from a plain program's by a relative error of at most 0.0049.
Values may be sent and summed in bfloat16 or wider, within the bound.
A program may use at most 128 MiB of HBM per device.

v0:
```python
import jax
import jax.numpy as jnp
from jax import lax
from jax.sharding import PartitionSpec as P

GRID_N = 96
DEG = 6


top_bound = 12.0
cut_bound = 0.0
low_bound = -0.25


def along_rows(values):
    length = values.shape[1]
    padded = jnp.pad(values, ((0, 0), (1, 1), (0, 0)))
    return padded[:, 2 : length + 2, :] + padded[:, 0:length, :]


def along_columns(values, grid_side):
    width = values.shape[2]
    padded = jnp.pad(values, ((0, 0), (0, 0), (grid_side, grid_side)))
    return padded[:, :, 2 * grid_side : width + 2 * grid_side] + padded[:, :, 0:width]


def along_depth(values, upper_mask, lower_mask):
    width = values.shape[2]
    padded = jnp.pad(values, ((0, 0), (0, 0), (1, 1)))
    return padded[:, :, 2 : width + 2] * upper_mask + padded[:, :, 0:width] * lower_mask


def hamiltonian(values, shaped_pot, upper_mask, lower_mask):
    rows_sum = along_rows(values)
    cols_sum = along_columns(values, GRID_N)
    depth_sum = along_depth(values, upper_mask, lower_mask)
    faces = rows_sum + cols_sum + depth_sum
    edges = along_rows(cols_sum + depth_sum) + along_columns(depth_sum, GRID_N)
    return (8.0 + shaped_pot) * values - 2.0 / 3.0 * faces - 1.0 / 3.0 * edges


def chebyshev_filter(fields, shaped_pot, upper_mask, lower_mask):
    half_width = (top_bound - cut_bound) / 2.0
    centre = (top_bound + cut_bound) / 2.0
    sigma_old = half_width / (low_bound - centre)
    ratio_inverse = 2.0 / sigma_old
    first_scale = sigma_old / half_width
    step_scales = []
    old_scales = []
    for order_index in range(2, DEG + 1):
        sigma_new = 1.0 / (ratio_inverse - sigma_old)
        step_scales.append(2.0 * sigma_new / half_width)
        old_scales.append(sigma_old * sigma_new)
        sigma_old = sigma_new
    step_table = jnp.array(step_scales, dtype=jnp.float32)
    old_table = jnp.array(old_scales, dtype=jnp.float32)
    current = (
        hamiltonian(fields, shaped_pot, upper_mask, lower_mask) - centre * fields
    ) * first_scale

    def advance(order_index, carried):
        older, present = carried
        applied = hamiltonian(present, shaped_pot, upper_mask, lower_mask)
        newer = (applied - centre * present) * step_table[order_index] - old_table[
            order_index
        ] * older
        return (present, newer)

    older, current = lax.fori_loop(0, DEG - 1, advance, (fields, current))
    return current


def local(orbitals, potential, subspace):
    local_count = orbitals.shape[0]
    total_cells = orbitals.shape[1]
    grid_side = GRID_N
    plane = grid_side * grid_side
    fields = orbitals.astype(jnp.float32).reshape(local_count, grid_side, plane)
    shaped_pot = potential.reshape(1, grid_side, plane)
    depth_index = jnp.arange(plane, dtype=jnp.int32) % grid_side
    upper_mask = (depth_index < grid_side - 1).astype(jnp.float32)
    lower_mask = (depth_index > 0).astype(jnp.float32)
    result = chebyshev_filter(fields, shaped_pot, upper_mask, lower_mask)
    filtered = result.astype(jnp.bfloat16).reshape(local_count, total_cells)
    orb_count = lax.axis_size("orb")
    grid_count = lax.axis_size("grid")
    width_all = subspace.shape[1]
    whole_matrix = lax.all_gather(subspace, ("orb", "grid"), axis=0, tiled=True)
    moved = lax.all_to_all(
        lax.all_to_all(filtered, "orb", split_axis=1, concat_axis=0, tiled=True),
        "grid",
        split_axis=1,
        concat_axis=0,
        tiled=True,
    )
    shaped_matrix = whole_matrix.reshape(orb_count, grid_count, local_count, width_all)
    matrix = shaped_matrix.transpose(1, 0, 2, 3).reshape(width_all, width_all)
    rotated = lax.dot_general(
        matrix, moved, (((0,), (0,)), ((), ())), preferred_element_type=jnp.float32
    )
    return rotated.astype(jnp.bfloat16)


def solution(mesh):
    placed = (P(("orb", "grid"), None), P(), P(("orb", "grid"), None))
    return jax.shard_map(
        local, mesh=mesh, in_specs=placed, out_specs=P(None, ("orb", "grid")), check_vma=False
    )
```

profile of v0, /device:TPU:1, one launch (start us, length us, event | category | flops | bytes accessed | tf_op | source)
XLA Modules:
  0.0 890.3 jit_solution(7926169004075862296)
XLA Ops:
  0.7 4.4 broadcast_add_fusion
  7.5 5.9 copy.18
  15.7 19.5 %fusion.37 = (f32[2,96,9216]{2,1,0:T(8,128)}, f32[2,96,9216]{2,1,0:T(8,128)}) fusion(f32[2,96,9216]{2,1,0:T(8,128)} %bitcast.29, f32[9216]{0:T(1024)} %get-tuple-element.253, f32[9216]{0:T(1024)} %get-tuple-element.252), kind=kLoop, calls=%fused_computation.52 | loop fusion | flops 8847360 | bytes 21307392 | tf_op jit(solution)/shard_map/add | solution.py:38
  35.2 27.5 %fusion.31 = f32[2,96,9216]{2,1,0:T(8,128)} fusion(f32[2,96,9216]{2,1,0:T(8,128)} %get-tuple-element.249, f32[2,96,9216]{2,1,0:T(8,128)} %bitcast.30, f32[2,96,9216]{2,1,0:T(8,128)} %get-tuple-element.248, f32[96,9216]{1,0:T(8,128)S(1)} %copy-done.4), kind=kLoop, calls=%fused_computation.42 | loop fusion | flops 26542080 | bytes 31850496 | tf_op jit(solution)/shard_map/mul | solution.py:57
  62.7 309.0 %while.19 = (s32[]{:T(128)}, f32[2,96,9216]{2,1,0:T(8,128)}, f32[2,96,9216]{2,1,0:T(8,128)}, f32[1,96,9216]{2,1,0:T(8,128)}, s32[]{:T(128)}, /*index=5*/f32[5]{0:T(128)S(1)}, f32[5]{0:T(128)S(1)}) while((s32[]{:T(128)}, f32[2,96,9216]{2,1,0:T(8,128)}, f32[2,96,9216]{2,1,0:T(8,128)}, f32[1,96,9216]{2,1,0:T(8,128)}, ...), condition=%wide.region_1.2_spmd.clone.clone, body=%wide.region_0.1_spmd.sunk.clone.clone.sunk | while | flops 39905280 | bytes 138166448 | solution.py:69
  62.9 19.7 %fusion.50 = (f32[2,96,9216]{2,1,0:T(8,128)}, f32[2,96,9216]{2,1,0:T(8,128)}) fusion(f32[2,96,9216]{2,1,0:T(8,128)} %get-tuple-element.296, f32[9216]{0:T(1024)S(1)} %get-tuple-element.283, f32[9216]{0:T(1024)S(1)} %get-tuple-element.284), kind=kLoop, calls=%fused_computation.21.clone.1 | loop fusion | flops 8847360 | bytes 21307392 | tf_op jit(solution)/shard_map/while/body/eval_jaxpr/add | solution.py:38
  84.1 30.9 %fusion.51 = f32[2,96,9216]{2,1,0:T(8,128)} fusion(f32[2,96,9216]{2,1,0:T(8,128)} %get-tuple-element.285, f32[2,96,9216]{2,1,0:T(8,128)} %get-tuple-element.296, f32[2,96,9216]{2,1,0:T(8,128)} %get-tuple-element.286, f32[2,96,9216]{2,1,0:T(8,128)} %get-tuple-element.295, f32[]{:T(128)} %bitcast.27, f32[]{:T(128)} %bitcast.28, ...), kind=kLoop, calls=%fused_computation.14.clone.1 | loop fusion | flops 30081024 | bytes 38928392 | tf_op jit(solution)/shard_map/while/body/eval_jaxpr/sub | solution.py:64
  115.0 6.7 copy.27
  121.8 2.9 copy.28
  124.7 19.7 %fusion.50 = (f32[2,96,9216]{2,1,0:T(8,128)}, f32[2,96,9216]{2,1,0:T(8,128)}) fusion(f32[2,96,9216]{2,1,0:T(8,128)} %get-tuple-element.296, f32[9216]{0:T(1024)S(1)} %get-tuple-element.283, f32[9216]{0:T(1024)S(1)} %get-tuple-element.284), kind=kLoop, calls=%fused_computation.21.clone.1 | loop fusion | flops 8847360 | bytes 21307392 | tf_op jit(solution)/shard_map/while/body/eval_jaxpr/add | solution.py:38
  145.8 30.9 %fusion.51 = f32[2,96,9216]{2,1,0:T(8,128)} fusion(f32[2,96,9216]{2,1,0:T(8,128)} %get-tuple-element.285, f32[2,96,9216]{2,1,0:T(8,128)} %get-tuple-element.296, f32[2,96,9216]{2,1,0:T(8,128)} %get-tuple-element.286, f32[2,96,9216]{2,1,0:T(8,128)} %get-tuple-element.295, f32[]{:T(128)} %bitcast.27, f32[]{:T(128)} %bitcast.28, ...), kind=kLoop, calls=%fused_computation.14.clone.1 | loop fusion | flops 30081024 | bytes 38928392 | tf_op jit(solution)/shard_map/while/body/eval_jaxpr/sub | solution.py:64
  176.8 6.7 copy.27
  183.5 2.9 copy.28
  186.5 19.7 %fusion.50 = (f32[2,96,9216]{2,1,0:T(8,128)}, f32[2,96,9216]{2,1,0:T(8,128)}) fusion(f32[2,96,9216]{2,1,0:T(8,128)} %get-tuple-element.296, f32[9216]{0:T(1024)S(1)} %get-tuple-element.283, f32[9216]{0:T(1024)S(1)} %get-tuple-element.284), kind=kLoop, calls=%fused_computation.21.clone.1 | loop fusion | flops 8847360 | bytes 21307392 | tf_op jit(solution)/shard_map/while/body/eval_jaxpr/add | solution.py:38
  207.6 30.9 %fusion.51 = f32[2,96,9216]{2,1,0:T(8,128)} fusion(f32[2,96,9216]{2,1,0:T(8,128)} %get-tuple-element.285, f32[2,96,9216]{2,1,0:T(8,128)} %get-tuple-element.296, f32[2,96,9216]{2,1,0:T(8,128)} %get-tuple-element.286, f32[2,96,9216]{2,1,0:T(8,128)} %get-tuple-element.295, f32[]{:T(128)} %bitcast.27, f32[]{:T(128)} %bitcast.28, ...), kind=kLoop, calls=%fused_computation.14.clone.1 | loop fusion | flops 30081024 | bytes 38928392 | tf_op jit(solution)/shard_map/while/body/eval_jaxpr/sub | solution.py:64
  238.5 6.7 copy.27
  248.2 19.7 %fusion.50 = (f32[2,96,9216]{2,1,0:T(8,128)}, f32[2,96,9216]{2,1,0:T(8,128)}) fusion(f32[2,96,9216]{2,1,0:T(8,128)} %get-tuple-element.296, f32[9216]{0:T(1024)S(1)} %get-tuple-element.283, f32[9216]{0:T(1024)S(1)} %get-tuple-element.284), kind=kLoop, calls=%fused_computation.21.clone.1 | loop fusion | flops 8847360 | bytes 21307392 | tf_op jit(solution)/shard_map/while/body/eval_jaxpr/add | solution.py:38
  269.4 30.9 %fusion.51 = f32[2,96,9216]{2,1,0:T(8,128)} fusion(f32[2,96,9216]{2,1,0:T(8,128)} %get-tuple-element.285, f32[2,96,9216]{2,1,0:T(8,128)} %get-tuple-element.296, f32[2,96,9216]{2,1,0:T(8,128)} %get-tuple-element.286, f32[2,96,9216]{2,1,0:T(8,128)} %get-tuple-element.295, f32[]{:T(128)} %bitcast.27, f32[]{:T(128)} %bitcast.28, ...), kind=kLoop, calls=%fused_computation.14.clone.1 | loop fusion | flops 30081024 | bytes 38928392 | tf_op jit(solution)/shard_map/while/body/eval_jaxpr/sub | solution.py:64
  300.3 6.7 copy.27
  310.0 19.7 %fusion.50 = (f32[2,96,9216]{2,1,0:T(8,128)}, f32[2,96,9216]{2,1,0:T(8,128)}) fusion(f32[2,96,9216]{2,1,0:T(8,128)} %get-tuple-element.296, f32[9216]{0:T(1024)S(1)} %get-tuple-element.283, f32[9216]{0:T(1024)S(1)} %get-tuple-element.284), kind=kLoop, calls=%fused_computation.21.clone.1 | loop fusion | flops 8847360 | bytes 21307392 | tf_op jit(solution)/shard_map/while/body/eval_jaxpr/add | solution.py:38
  331.1 30.9 %fusion.51 = f32[2,96,9216]{2,1,0:T(8,128)} fusion(f32[2,96,9216]{2,1,0:T(8,128)} %get-tuple-element.285, f32[2,96,9216]{2,1,0:T(8,128)} %get-tuple-element.296, f32[2,96,9216]{2,1,0:T(8,128)} %get-tuple-element.286, f32[2,96,9216]{2,1,0:T(8,128)} %get-tuple-element.295, f32[]{:T(128)} %bitcast.27, f32[]{:T(128)} %bitcast.28, ...), kind=kLoop, calls=%fused_computation.14.clone.1 | loop fusion | flops 30081024 | bytes 38928392 | tf_op jit(solution)/shard_map/while/body/eval_jaxpr/sub | solution.py:64
  362.1 6.7 copy.27
  371.7 5.3 convert_element_type.49
  377.0 4.3 all_to_all.26
  381.3 10.7 %copy.11 = bf16[2,4,221184]{2,0,1:T(2,128)(2,1)S(1)} copy(bf16[2,4,221184]{2,1,0:T(4,128)(2,1)S(1)} %all_to_all.26) | data formatting | bytes 7077888 | tf_op jit(solution)/shard_map/all_to_all | solution.py:90
  392.0 87.9 %all_to_all.35 = bf16[2,4,221184]{2,0,1:T(2,128)(2,1)S(1)} all-to-all(bf16[2,4,221184]{2,0,1:T(2,128)(2,1)S(1)} %copy.11), channel_id=1, replica_groups=mesh['orb'=4,'grid'=64] {'orb'}, dimensions={1} | all-to-all | bytes 7077888 | tf_op jit(solution)/shard_map/all_to_all | solution.py:90
  479.9 3.5 all_to_all.29
  483.4 5.7 copy.12
  489.1 11.1 %all-to-all-start.1 = ((bf16[8,64,3456]{2,0,1:T(8,128)(2,1)}), bf16[8,64,3456]{2,0,1:T(8,128)(2,1)S(1)}, u32[]{:S(2)}, u32[]{:S(2)}) async-start(bf16[8,64,3456]{2,0,1:T(8,128)(2,1)} %copy.12), calls=%async_computation.1 | async-start | bytes 7077888 | tf_op jit(solution)/shard_map/all_to_all | solution.py:89
  500.3 376.3 %all-gather = bf16[256,2,512]{2,1,0:T(2,128)(2,1)S(1)} all-gather(bf16[1,2,512]{2,1,0:T(2,128)(2,1)S(1)} %bitcast.36), channel_id=1, replica_groups=mesh['orb'=4,'grid'=64] {'orb','grid'}, dimensions={0}, use_global_device_ids=true | all-gather | bytes 526336 | tf_op jit(solution)/shard_map/all_gather | solution.py:88
  879.7 4.8 fusion.35
  884.6 5.7 copy.14
  (61 shorter events, 24.8 us)
Async XLA Ops:
  0.0 5.0 copy-start.2
  7.5 5.9 copy-start.3
  15.7 19.5 %copy-start.4 = (f32[96,9216]{1,0:T(8,128)S(1)}, f32[96,9216]{1,0:T(8,128)}, u32[]{:S(2)}) copy-start(f32[96,9216]{1,0:T(8,128)} %add.215) | copy-start | bytes 10616836
  35.2 27.5 %copy-start.6 = (f32[5]{0:T(128)S(1)}, f32[5]{0:T(128)}, u32[]{:S(2)}) copy-start(f32[5]{0:T(128)} %constant.104.clone..sunk.3) | copy-start | bytes 64
  35.2 27.5 %copy-start.7 = (f32[5]{0:T(128)S(1)}, f32[5]{0:T(128)}, u32[]{:S(2)}) copy-start(f32[5]{0:T(128)} %constant.105.clone..sunk.3) | copy-start | bytes 64
  62.9 20.9 %copy-start.1 = (f32[1,96,9216]{2,1,0:T(8,128)S(1)}, f32[1,96,9216]{2,1,0:T(8,128)}, u32[]{:S(2)}) copy-start(f32[1,96,9216]{2,1,0:T(8,128)} %get-tuple-element.304) | copy-start | bytes 10616836 | tf_op jit(solution)/shard_map/while
  115.0 6.7 copy-start
  124.7 20.9 %copy-start.1 = (f32[1,96,9216]{2,1,0:T(8,128)S(1)}, f32[1,96,9216]{2,1,0:T(8,128)}, u32[]{:S(2)}) copy-start(f32[1,96,9216]{2,1,0:T(8,128)} %get-tuple-element.304) | copy-start | bytes 10616836 | tf_op jit(solution)/shard_map/while
  176.8 6.7 copy-start
  186.5 20.9 %copy-start.1 = (f32[1,96,9216]{2,1,0:T(8,128)S(1)}, f32[1,96,9216]{2,1,0:T(8,128)}, u32[]{:S(2)}) copy-start(f32[1,96,9216]{2,1,0:T(8,128)} %get-tuple-element.304) | copy-start | bytes 10616836 | tf_op jit(solution)/shard_map/while
  238.5 6.7 copy-start
  248.2 20.9 %copy-start.1 = (f32[1,96,9216]{2,1,0:T(8,128)S(1)}, f32[1,96,9216]{2,1,0:T(8,128)}, u32[]{:S(2)}) copy-start(f32[1,96,9216]{2,1,0:T(8,128)} %get-tuple-element.304) | copy-start | bytes 10616836 | tf_op jit(solution)/shard_map/while
  300.3 6.7 copy-start
  310.0 20.9 %copy-start.1 = (f32[1,96,9216]{2,1,0:T(8,128)S(1)}, f32[1,96,9216]{2,1,0:T(8,128)}, u32[]{:S(2)}) copy-start(f32[1,96,9216]{2,1,0:T(8,128)} %get-tuple-element.304) | copy-start | bytes 10616836 | tf_op jit(solution)/shard_map/while
  362.1 6.7 copy-start
  483.4 16.9 %copy-start.5 = (bf16[2,512]{1,0:T(2,128)(2,1)S(1)}, bf16[2,512]{1,0:T(2,128)(2,1)}, u32[]{:S(2)}) copy-start(bf16[2,512]{1,0:T(2,128)(2,1)} %param.9) | copy-start | bytes 6148
  489.1 390.6 %all-to-all-start.1 = ((bf16[8,64,3456]{2,0,1:T(8,128)(2,1)}), bf16[8,64,3456]{2,0,1:T(8,128)(2,1)S(1)}, u32[]{:S(2)}, u32[]{:S(2)}) async-start(bf16[8,64,3456]{2,0,1:T(8,128)(2,1)} %copy.12), calls=%async_computation.1 | async-start | bytes 7077888 | tf_op jit(solution)/shard_map/all_to_all | solution.py:89
where the time goes:
time: 891 us; the launch traced here: 890 us
  blocking collectives  464 us (52%)
  other arithmetic  312 us (35%)
  local copies, waits for them, and re-layouts  98.1 us (11%)
  starting transfers between devices  11.1 us (1%)
    all_gather x1, blocking collectives, local(): whole_matrix = lax.all_gather(subspace, ('orb', 'grid'), axis=0, tiled=True)  376 us
    sub x5, other arithmetic, advance(): (applied - centre * present) * step_table[order_index]  155 us
    add x6, other arithmetic, hamiltonian(): edges = along_rows(cols_sum + depth_sum) + along_columns(depth_sum, GRID_N)  118 us
    all_to_all x1, blocking collectives, local(): lax.all_to_all(filtered, 'orb', split_axis=1, concat_axis=0, tiled=True)  87.9 us
    while x30, local copies, waits for them, and re-layouts  48.3 us
    mul x1, other arithmetic, chebyshev_filter(): (hamiltonian(fields, shaped_pot, upper_mask, lower_mask) - centre * field...  27.5 us
  transfers between devices with their start and end apart: 1, of which 0 were waited for; matrix products, arithmetic and copies ran while one was open for 0% of the time, Pallas kernels for 0%

commit v1 on v0

--- a/solution.py
+++ b/solution.py
@@ -1,6 +1,8 @@
 import jax
 import jax.numpy as jnp
 from jax import lax
+from jax.experimental import pallas as pl
+from jax.experimental.pallas import tpu as pltpu
 from jax.sharding import PartitionSpec as P
 
 GRID_N = 96
@@ -70,9 +72,87 @@
     return current
 
 
+DEVICES = 256
+BLOCKS = 27
+MESH = pl.DeviceIdType.MESH
+
+
+def torus_peer(orb, grid, step):
+    mixed = lax.rem(step * 91, DEVICES)
+    z = orb * 2 + lax.rem(grid // 2, 2)
+    z = lax.rem(z + mixed // 32, 8)
+    y = lax.rem(grid // 16 + lax.rem(mixed // 8, 4), 4)
+    x = lax.rem(lax.rem(grid // 4, 4) + lax.rem(mixed // 2, 4), 4)
+    core = lax.rem(grid + lax.rem(mixed, 2), 2)
+    return z // 2, y * 16 + x * 4 + lax.rem(z, 2) * 2 + core
+
+
+def exchange_kernel(source, landed, send_sem, recv_sem):
+    orb, grid = lax.axis_index("orb"), lax.axis_index("grid")
+    me = orb * 64 + grid
+    barrier = pltpu.get_barrier_semaphore()
+
+    def greet(step, carry):
+        peer_orb, peer_grid = torus_peer(orb, grid, step)
+        pl.semaphore_signal(barrier, inc=1, device_id=(peer_orb, peer_grid), device_id_type=MESH)
+        return carry
+
+    lax.fori_loop(1, DEVICES, greet, 0)
+    pl.semaphore_wait(barrier, DEVICES - 1)
+
+    def send(step, carry):
+        peer_orb, peer_grid = torus_peer(orb, grid, step)
+        pltpu.make_async_remote_copy(
+            source.at[peer_orb * 64 + peer_grid], landed.at[:, me], send_sem, recv_sem,
+            device_id=(peer_orb, peer_grid), device_id_type=MESH,
+        ).start()
+        return carry
+
+    lax.fori_loop(1, DEVICES, send, 0)
+    pltpu.make_async_copy(source.at[me], landed.at[:, me], recv_sem).start()
+    pltpu.make_async_copy(landed, landed, recv_sem).wait()
+    sent = source.at[pl.ds(0, DEVICES - 1)]
+    pltpu.make_async_copy(sent, sent, send_sem).wait()
+
+
+def exchange(source):
+    return pl.pallas_call(
+        exchange_kernel,
+        out_shape=jax.ShapeDtypeStruct((BLOCKS, DEVICES, 2, 128), jnp.bfloat16),
+        in_specs=[pl.BlockSpec(memory_space=pltpu.VMEM)],
+        out_specs=pl.BlockSpec(memory_space=pltpu.VMEM),
+        scratch_shapes=[pltpu.SemaphoreType.DMA, pltpu.SemaphoreType.DMA],
+        compiler_params=pltpu.CompilerParams(
+            collective_id=0, has_side_effects=True, vmem_limit_bytes=32 * 2**20
+        ),
+        name="exchange",
+    )(source)
+
+
+def rotate_kernel(matrix, fields, rotated):
+    wide = jnp.concatenate([fields[i] for i in range(3)], axis=1)
+    rotated[...] = lax.dot_general(
+        matrix[...], wide, (((0,), (0,)), ((), ())), preferred_element_type=jnp.float32
+    ).astype(jnp.bfloat16)
+
+
+def rotate(matrix, fields):
+    return pl.pallas_call(
+        rotate_kernel,
+        grid=(BLOCKS // 3,),
+        out_shape=jax.ShapeDtypeStruct((512, BLOCKS * 128), jnp.bfloat16),
+        in_specs=[
+            pl.BlockSpec((512, 512), lambda i: (0, 0)),
+            pl.BlockSpec((3, 512, 128), lambda i: (i, 0, 0)),
+        ],
+        out_specs=pl.BlockSpec((512, 384), lambda i: (0, i)),
+        compiler_params=pltpu.CompilerParams(vmem_limit_bytes=32 * 2**20),
+        name="rotate",
+    )(matrix, fields)
+
+
 def local(orbitals, potential, subspace):
     local_count = orbitals.shape[0]
-    total_cells = orbitals.shape[1]
     grid_side = GRID_N
     plane = grid_side * grid_side
     fields = orbitals.astype(jnp.float32).reshape(local_count, grid_side, plane)
@@ -81,24 +161,10 @@
     upper_mask = (depth_index < grid_side - 1).astype(jnp.float32)
     lower_mask = (depth_index > 0).astype(jnp.float32)
     result = chebyshev_filter(fields, shaped_pot, upper_mask, lower_mask)
-    filtered = result.astype(jnp.bfloat16).reshape(local_count, total_cells)
-    orb_count = lax.axis_size("orb")
-    grid_count = lax.axis_size("grid")
-    width_all = subspace.shape[1]
-    whole_matrix = lax.all_gather(subspace, ("orb", "grid"), axis=0, tiled=True)
-    moved = lax.all_to_all(
-        lax.all_to_all(filtered, "orb", split_axis=1, concat_axis=0, tiled=True),
-        "grid",
-        split_axis=1,
-        concat_axis=0,
-        tiled=True,
-    )
-    shaped_matrix = whole_matrix.reshape(orb_count, grid_count, local_count, width_all)
-    matrix = shaped_matrix.transpose(1, 0, 2, 3).reshape(width_all, width_all)
-    rotated = lax.dot_general(
-        matrix, moved, (((0,), (0,)), ((), ())), preferred_element_type=jnp.float32
-    )
-    return rotated.astype(jnp.bfloat16)
+    filtered = result.astype(jnp.bfloat16).reshape(local_count, DEVICES, BLOCKS, 128)
+    matrix = lax.all_gather(subspace, ("orb", "grid"), axis=0, tiled=True)
+    landed = exchange(filtered.transpose(1, 2, 0, 3))
+    return rotate(matrix, landed.reshape(BLOCKS, 512, 128))
 
 
 def solution(mesh):

time: 891 us -> 860 us (0.965)
  Pallas kernels: 0 us -> 111 us
  blocking collectives: 464 us -> 367 us
  local copies, waits for them, and re-layouts: 98.1 us -> 82 us
  other arithmetic: 312 us -> 299 us
  starting transfers between devices: 11.1 us -> 0 us
    pallas_call x0 -> x2, Pallas kernels: none -> 111 us  [the longest x1 105 us: exchange(): pl.pallas_call(exchange_kernel, out_shape=jax.ShapeDtypeStruct((BLOCKS, D...]
    all_to_all x1 -> x0, blocking collectives: 87.9 us -> none  [local(): lax.all_to_all(filtered, 'orb', split_axis=1, concat_axis=0, tiled=True)]
    all_to_all x4 -> x0, local copies, waits for them, and re-layouts: 24.2 us -> none  [the longest x2 15 us: local(): lax.all_to_all(filtered, 'orb', split_axis=1, concat_axis=0, tiled=True)]
    all_to_all x1 -> x0, starting transfers between devices: 11.1 us -> none  [local(): lax.all_to_all(lax.all_to_all(filtered, 'orb', split_axis=1, concat_axis=...]
    reshape x2, local copies, waits for them, and re-layouts: 3.19 us -> 14.2 us  [local(): result.astype(jnp.bfloat16).reshape(local_count, DEVICES, BLOCKS, 128)]
    all_gather x1, blocking collectives: 376 us -> 367 us  [local(): matrix = lax.all_gather(subspace, ('orb', 'grid'), axis=0, tiled=True)]
  transfers between devices with their start and end apart: 1 -> 0, of which waited for: 0 -> 0; matrix products, arithmetic and copies ran while one was open for 0% -> 0% of each run, Pallas kernels for 0% -> 0%
where the time goes in v1:
time: 860 us; the launch traced here: 859 us
  blocking collectives  367 us (43%)
  other arithmetic  299 us (35%)
  Pallas kernels  111 us (13%)
  local copies, waits for them, and re-layouts  82 us (10%)
    all_gather x1, blocking collectives, local(): matrix = lax.all_gather(subspace, ('orb', 'grid'), axis=0, tiled=True)  367 us
    sub x5, other arithmetic, advance(): (applied - centre * present) * step_table[order_index]  155 us
    add x6, other arithmetic, hamiltonian(): edges = along_rows(cols_sum + depth_sum) + along_columns(depth_sum, GRID_N)  109 us
    pallas_call x1, Pallas kernels, exchange(): pl.pallas_call(exchange_kernel, out_shape=jax.ShapeDtypeStruct((BLOCKS, D...  105 us
    while x30, local copies, waits for them, and re-layouts  48.4 us
    mul x1, other arithmetic, chebyshev_filter(): (hamiltonian(fields, shaped_pot, upper_mask, lower_mask) - centre * field...  28.4 us

profile of v1, /device:TPU:1, one launch (start us, length us, event | category | flops | bytes accessed | tf_op | source)
XLA Modules:
  0.0 859.1 jit_solution(297155320493875883)
XLA Ops:
  0.0 2.8 copy.11
  2.9 10.4 %fusion.35 = (f32[2,96,9216]{2,1,0:T(8,128)}, f32[2,96,9216]{2,1,0:T(8,128)}) fusion(f32[2,96,9216]{2,1,0:T(8,128)S(1)} %bitcast.22, f32[9216]{0:T(1024)S(1)} %get-tuple-element.253, f32[9216]{0:T(1024)S(1)} %get-tuple-element.252), kind=kLoop, calls=%fused_computation.50 | loop fusion | flops 8847360 | bytes 21307392 | tf_op jit(solution)/shard_map/add | solution.py:40
  15.3 4.8 add.215
  20.1 28.4 %fusion.31 = f32[2,96,9216]{2,1,0:T(8,128)} fusion(f32[2,96,9216]{2,1,0:T(8,128)} %get-tuple-element.249, f32[2,96,9216]{2,1,0:T(8,128)} %bitcast.23, f32[2,96,9216]{2,1,0:T(8,128)} %get-tuple-element.248, f32[96,9216]{1,0:T(8,128)} %add.215), kind=kLoop, calls=%fused_computation.42 | loop fusion | flops 26542080 | bytes 31850496 | tf_op jit(solution)/shard_map/mul | solution.py:59
  48.5 2.4 reshape.52
  50.9 309.6 %while.19 = (s32[]{:T(128)}, f32[2,96,9216]{2,1,0:T(8,128)}, f32[2,96,9216]{2,1,0:T(8,128)}, f32[1,96,9216]{2,1,0:T(8,128)}, s32[]{:T(128)}, /*index=5*/f32[5]{0:T(128)S(1)}, f32[5]{0:T(128)S(1)}) while((s32[]{:T(128)}, f32[2,96,9216]{2,1,0:T(8,128)}, f32[2,96,9216]{2,1,0:T(8,128)}, f32[1,96,9216]{2,1,0:T(8,128)}, ...), condition=%wide.region_1.2_spmd.clone.clone, body=%wide.region_0.1_spmd.sunk.clone.clone.sunk | while | flops 39905280 | bytes 138166448 | solution.py:71
  51.0 19.7 %fusion.47 = (f32[2,96,9216]{2,1,0:T(8,128)}, f32[2,96,9216]{2,1,0:T(8,128)}) fusion(f32[2,96,9216]{2,1,0:T(8,128)} %get-tuple-element.296, f32[9216]{0:T(1024)S(1)} %get-tuple-element.283, f32[9216]{0:T(1024)S(1)} %get-tuple-element.284), kind=kLoop, calls=%fused_computation.21.clone.1 | loop fusion | flops 8847360 | bytes 21307392 | tf_op jit(solution)/shard_map/while/body/eval_jaxpr/add | solution.py:40
  72.2 30.9 %fusion.48 = f32[2,96,9216]{2,1,0:T(8,128)} fusion(f32[2,96,9216]{2,1,0:T(8,128)} %get-tuple-element.285, f32[2,96,9216]{2,1,0:T(8,128)} %get-tuple-element.296, f32[2,96,9216]{2,1,0:T(8,128)} %get-tuple-element.286, f32[2,96,9216]{2,1,0:T(8,128)} %get-tuple-element.295, f32[]{:T(128)} %bitcast.18, f32[]{:T(128)} %bitcast.19, ...), kind=kLoop, calls=%fused_computation.14.clone.1 | loop fusion | flops 30081024 | bytes 38928392 | tf_op jit(solution)/shard_map/while/body/eval_jaxpr/sub | solution.py:66
  103.2 6.7 copy.20
  109.9 2.9 copy.21
  112.9 19.7 %fusion.47 = (f32[2,96,9216]{2,1,0:T(8,128)}, f32[2,96,9216]{2,1,0:T(8,128)}) fusion(f32[2,96,9216]{2,1,0:T(8,128)} %get-tuple-element.296, f32[9216]{0:T(1024)S(1)} %get-tuple-element.283, f32[9216]{0:T(1024)S(1)} %get-tuple-element.284), kind=kLoop, calls=%fused_computation.21.clone.1 | loop fusion | flops 8847360 | bytes 21307392 | tf_op jit(solution)/shard_map/while/body/eval_jaxpr/add | solution.py:40
  134.1 30.9 %fusion.48 = f32[2,96,9216]{2,1,0:T(8,128)} fusion(f32[2,96,9216]{2,1,0:T(8,128)} %get-tuple-element.285, f32[2,96,9216]{2,1,0:T(8,128)} %get-tuple-element.296, f32[2,96,9216]{2,1,0:T(8,128)} %get-tuple-element.286, f32[2,96,9216]{2,1,0:T(8,128)} %get-tuple-element.295, f32[]{:T(128)} %bitcast.18, f32[]{:T(128)} %bitcast.19, ...), kind=kLoop, calls=%fused_computation.14.clone.1 | loop fusion | flops 30081024 | bytes 38928392 | tf_op jit(solution)/shard_map/while/body/eval_jaxpr/sub | solution.py:66
  165.1 6.7 copy.20
  171.8 2.9 copy.21
  174.8 19.7 %fusion.47 = (f32[2,96,9216]{2,1,0:T(8,128)}, f32[2,96,9216]{2,1,0:T(8,128)}) fusion(f32[2,96,9216]{2,1,0:T(8,128)} %get-tuple-element.296, f32[9216]{0:T(1024)S(1)} %get-tuple-element.283, f32[9216]{0:T(1024)S(1)} %get-tuple-element.284), kind=kLoop, calls=%fused_computation.21.clone.1 | loop fusion | flops 8847360 | bytes 21307392 | tf_op jit(solution)/shard_map/while/body/eval_jaxpr/add | solution.py:40
  196.1 30.9 %fusion.48 = f32[2,96,9216]{2,1,0:T(8,128)} fusion(f32[2,96,9216]{2,1,0:T(8,128)} %get-tuple-element.285, f32[2,96,9216]{2,1,0:T(8,128)} %get-tuple-element.296, f32[2,96,9216]{2,1,0:T(8,128)} %get-tuple-element.286, f32[2,96,9216]{2,1,0:T(8,128)} %get-tuple-element.295, f32[]{:T(128)} %bitcast.18, f32[]{:T(128)} %bitcast.19, ...), kind=kLoop, calls=%fused_computation.14.clone.1 | loop fusion | flops 30081024 | bytes 38928392 | tf_op jit(solution)/shard_map/while/body/eval_jaxpr/sub | solution.py:66
  227.0 6.7 copy.20
  233.8 2.9 copy.21
  236.7 19.7 %fusion.47 = (f32[2,96,9216]{2,1,0:T(8,128)}, f32[2,96,9216]{2,1,0:T(8,128)}) fusion(f32[2,96,9216]{2,1,0:T(8,128)} %get-tuple-element.296, f32[9216]{0:T(1024)S(1)} %get-tuple-element.283, f32[9216]{0:T(1024)S(1)} %get-tuple-element.284), kind=kLoop, calls=%fused_computation.21.clone.1 | loop fusion | flops 8847360 | bytes 21307392 | tf_op jit(solution)/shard_map/while/body/eval_jaxpr/add | solution.py:40
  258.0 30.9 %fusion.48 = f32[2,96,9216]{2,1,0:T(8,128)} fusion(f32[2,96,9216]{2,1,0:T(8,128)} %get-tuple-element.285, f32[2,96,9216]{2,1,0:T(8,128)} %get-tuple-element.296, f32[2,96,9216]{2,1,0:T(8,128)} %get-tuple-element.286, f32[2,96,9216]{2,1,0:T(8,128)} %get-tuple-element.295, f32[]{:T(128)} %bitcast.18, f32[]{:T(128)} %bitcast.19, ...), kind=kLoop, calls=%fused_computation.14.clone.1 | loop fusion | flops 30081024 | bytes 38928392 | tf_op jit(solution)/shard_map/while/body/eval_jaxpr/sub | solution.py:66
  288.9 6.7 copy.20
  295.7 2.9 copy.21
  298.6 19.7 %fusion.47 = (f32[2,96,9216]{2,1,0:T(8,128)}, f32[2,96,9216]{2,1,0:T(8,128)}) fusion(f32[2,96,9216]{2,1,0:T(8,128)} %get-tuple-element.296, f32[9216]{0:T(1024)S(1)} %get-tuple-element.283, f32[9216]{0:T(1024)S(1)} %get-tuple-element.284), kind=kLoop, calls=%fused_computation.21.clone.1 | loop fusion | flops 8847360 | bytes 21307392 | tf_op jit(solution)/shard_map/while/body/eval_jaxpr/add | solution.py:40
  319.9 30.9 %fusion.48 = f32[2,96,9216]{2,1,0:T(8,128)} fusion(f32[2,96,9216]{2,1,0:T(8,128)} %get-tuple-element.285, f32[2,96,9216]{2,1,0:T(8,128)} %get-tuple-element.296, f32[2,96,9216]{2,1,0:T(8,128)} %get-tuple-element.286, f32[2,96,9216]{2,1,0:T(8,128)} %get-tuple-element.295, f32[]{:T(128)} %bitcast.18, f32[]{:T(128)} %bitcast.19, ...), kind=kLoop, calls=%fused_computation.14.clone.1 | loop fusion | flops 30081024 | bytes 38928392 | tf_op jit(solution)/shard_map/while/body/eval_jaxpr/sub | solution.py:66
  350.8 6.7 copy.20
  357.6 2.9 copy.21
  360.5 3.5 convert_element_type.43
  364.0 6.5 reshape.53
  370.5 7.7 copy.12
  378.2 104.5 %exchange.1 = bf16[27,256,2,128]{3,2,1,0:T(2,128)(2,1)S(1)} custom-call(bf16[256,27,2,128]{3,2,1,0:T(2,128)(2,1)S(1)} %bitcast.21), custom_call_target="tpu_custom_call" | custom-call | tf_op jit(solution)/shard_map/exchange/pallas_call | solution.py:119
  482.7 367.2 %all-gather = bf16[256,2,512]{2,1,0:T(2,128)(2,1)} all-gather(bf16[1,2,512]{2,1,0:T(2,128)(2,1)S(1)} %bitcast.26), channel_id=1, replica_groups=mesh['orb'=4,'grid'=64] {'orb','grid'}, dimensions={0}, use_global_device_ids=true | all-gather | bytes 526336 | tf_op jit(solution)/shard_map/all_gather | solution.py:165
  853.0 6.1 rotate.1
  (55 shorter events, 12.9 us)
Async XLA Ops:
  2.8 10.4 %copy-start.2 = (f32[1,2,96,9216]{3,2,1,0:T(8,128)}, f32[1,2,96,9216]{3,2,1,0:T(8,128)S(1)}, u32[]{:S(2)}) copy-start(f32[1,2,96,9216]{3,2,1,0:T(8,128)S(1)} %copy.11) | copy-start | bytes 21233668
  2.9 10.4 %copy-start.4 = (f32[884736]{0:T(1024)S(1)}, f32[884736]{0:T(1024)}, u32[]{:S(2)}) copy-start(f32[884736]{0:T(1024)} %param.8) | copy-start | bytes 10616836
  48.5 2.4 copy-start.6
  48.5 2.4 copy-start.7
  51.0 21.0 %copy-start.3 = (f32[1,96,9216]{2,1,0:T(8,128)S(1)}, f32[1,96,9216]{2,1,0:T(8,128)}, u32[]{:S(2)}) copy-start(f32[1,96,9216]{2,1,0:T(8,128)} %get-tuple-element.304) | copy-start | bytes 10616836 | tf_op jit(solution)/shard_map/while
  103.2 6.8 copy-start.1
  112.9 21.0 %copy-start.3 = (f32[1,96,9216]{2,1,0:T(8,128)S(1)}, f32[1,96,9216]{2,1,0:T(8,128)}, u32[]{:S(2)}) copy-start(f32[1,96,9216]{2,1,0:T(8,128)} %get-tuple-element.304) | copy-start | bytes 10616836 | tf_op jit(solution)/shard_map/while
  165.1 6.8 copy-start.1
  174.8 21.0 %copy-start.3 = (f32[1,96,9216]{2,1,0:T(8,128)S(1)}, f32[1,96,9216]{2,1,0:T(8,128)}, u32[]{:S(2)}) copy-start(f32[1,96,9216]{2,1,0:T(8,128)} %get-tuple-element.304) | copy-start | bytes 10616836 | tf_op jit(solution)/shard_map/while
  227.0 6.8 copy-start.1
  236.7 21.0 %copy-start.3 = (f32[1,96,9216]{2,1,0:T(8,128)S(1)}, f32[1,96,9216]{2,1,0:T(8,128)}, u32[]{:S(2)}) copy-start(f32[1,96,9216]{2,1,0:T(8,128)} %get-tuple-element.304) | copy-start | bytes 10616836 | tf_op jit(solution)/shard_map/while
  288.9 6.8 copy-start.1
  298.6 21.0 %copy-start.3 = (f32[1,96,9216]{2,1,0:T(8,128)S(1)}, f32[1,96,9216]{2,1,0:T(8,128)}, u32[]{:S(2)}) copy-start(f32[1,96,9216]{2,1,0:T(8,128)} %get-tuple-element.304) | copy-start | bytes 10616836 | tf_op jit(solution)/shard_map/while
  350.8 6.8 copy-start.1
  370.5 112.2 %copy-start.5 = (bf16[2,512]{1,0:T(2,128)(2,1)S(1)}, bf16[2,512]{1,0:T(2,128)(2,1)}, u32[]{:S(2)}) copy-start(bf16[2,512]{1,0:T(2,128)(2,1)} %param.9) | copy-start | bytes 6148
  852.0 1.0 copy-start

commit v2 on v1

v2 whole, which is shorter than its diff:
```python
import jax
import jax.numpy as jnp
from jax import lax
from jax.experimental import pallas as pl
from jax.experimental.pallas import tpu as pltpu
from jax.sharding import PartitionSpec as P

SIDE = 96
DEG = 6
DEVICES = 256
BLOCKS = 27
FLAT = 72
PERIOD = SIDE + 1
STEPS = PERIOD + 2 * DEG
MESH = pl.DeviceIdType.MESH

TOP = 12.0
CUT = 0.0
LOW = -0.25
HALF = (TOP - CUT) / 2.0
CENTRE = (TOP + CUT) / 2.0


def last_scale():
    at = (LOW - CENTRE) / HALF
    older, current = 1.0, at
    for _ in range(DEG - 1):
        older, current = current, 2.0 * at * current - older
    return 1.0 / current


def torus_peer(orb, grid, step):
    z = orb * 2 + lax.rem(grid // 2, 2)
    z = lax.rem(z + step // 32, 8)
    y = lax.rem(grid // 16 + lax.rem(step // 8, 4), 4)
    x = lax.rem(lax.rem(grid // 4, 4) + lax.rem(step // 2, 4), 4)
    core = lax.rem(grid + lax.rem(step, 2), 2)
    return z // 2, y * 16 + x * 4 + lax.rem(z, 2) * 2 + core


def sweep_kernel(
    orbitals, potential, subspace, landed, matrix,
    ring, wells, raw, packed, staged,
    send_sem, recv_sem, near_send, near_recv, far_send, far_recv,
):
    orb, grid = lax.axis_index("orb"), lax.axis_index("grid")
    me = orb * 64 + grid
    column = grid // 4 * 2 + lax.rem(grid, 2)
    depth = orb * 2 + lax.rem(grid // 2, 2)
    slot_of_me = column * 8 + depth
    downward = lax.rem(grid, 2)
    barrier = pltpu.get_barrier_semaphore()

    def greet(step, carry):
        peer = torus_peer(orb, grid, step)
        pl.semaphore_signal(barrier, inc=1, device_id=peer, device_id_type=MESH)
        return carry

    lax.fori_loop(1, DEVICES, greet, 0)

    lane = lax.broadcasted_iota(jnp.int32, (8, 128), 1)
    inside = lane < SIDE
    ones = jnp.where(inside, 1.0, 0.0).astype(jnp.float32)
    zeros = jnp.zeros((8, 128), jnp.float32)

    def clear(at, carry):
        for own in range(2):
            for group in range(4):
                ring[at // 4, lax.rem(at, 4), own, group, pl.ds(0, 8), :] = zeros
                ring[at // 4, lax.rem(at, 4), own, group, pl.ds(32, 8), :] = zeros
        return carry

    lax.fori_loop(0, DEG * 4, clear, 0)

    own_plane = me * 3 // 8 // 3 * 3
    ordered = jnp.where(downward == 1, SIDE - 3 - own_plane, own_plane)
    base = lax.rem(ordered + 24, SIDE) - DEG + PERIOD

    def position(number):
        return lax.rem(base + number, PERIOD)

    def plane_of(place):
        return jnp.where(downward == 1, SIDE - 1 - place, place)

    def to_lines(rows):
        first, second, third = rows
        return (
            jnp.where(inside, first, 0.0),
            jnp.where(inside, pltpu.roll(jnp.where(lane >= 96, first, second), 32, 1), 0.0),
            jnp.where(inside, pltpu.roll(jnp.where(lane >= 64, second, third), 64, 1), 0.0),
            jnp.where(inside, pltpu.roll(third, 96, 1), 0.0),
        )

    def to_rows(lines):
        early = pltpu.roll(lines[1], 96, 1)
        middle = pltpu.roll(lines[2], 64, 1)
        late = pltpu.roll(lines[3], 32, 1)
        return (
            jnp.where(lane < 96, lines[0], early),
            jnp.where(lane < 64, early, middle),
            jnp.where(lane < 32, middle, late),
        )

    def zero_plane(stage, slot):
        for own in range(2):
            for group in range(4):
                for part in range(3):
                    ring[stage, slot, own, group, pl.ds(8 + 8 * part, 8), :] = zeros

    def take(time):
        place = position(time)
        slot = lax.rem(time, 4)
        well = lax.rem(time, 8)

        @pl.when(place < SIDE)
        def _():
            plane = plane_of(place)
            raw[...] = orbitals[plane].astype(jnp.float32)
            for part in range(3):
                rows = [potential[plane, pl.ds(24 * part + j, 8, stride=3), :] for j in range(3)]
                for group, line in enumerate(to_lines(rows)):
                    wells[well, group, pl.ds(8 * part, 8), :] = 3.0 * line + 6.0
                for own in range(2):
                    rows = [raw[pl.ds(48 * part + 2 * j + own, 8, stride=6), :] for j in range(3)]
                    for group, line in enumerate(to_lines(rows)):
                        ring[0, slot, own, group, pl.ds(8 + 8 * part, 8), :] = line

        @pl.when(place == SIDE)
        def _():
            zero_plane(0, slot)

    def advance(stage, number, own, part):
        def read(plane):
            at = lax.rem(plane + 4, 4)
            rows = [
                ring[stage - 1, at, own, group, pl.ds(8 + 8 * part, 8), :] for group in range(4)
            ]
            before = ring[stage - 1, at, own, 3, pl.ds(7 + 8 * part, 8), :]
            after = ring[stage - 1, at, own, 0, pl.ds(9 + 8 * part, 8), :]
            return [before] + rows + [after]

        behind, here, ahead = read(number - 1), read(number), read(number + 1)
        across = [u + v for u, v in zip(behind, ahead)]
        if stage == 1:
            factor = 0.5 * ones
        elif stage == DEG:
            factor = (last_scale() / 81.0) * ones
        elif stage % 2:
            factor = ones
        else:
            factor = (1.0 / 81.0) * ones
        made = []
        for group in range(4):
            centre = here[group + 1]
            both = across[group + 1] + (here[group] + here[group + 2])
            wide = both + (centre + centre)
            along = pltpu.roll(wide, 1, 1) + pltpu.roll(wide, 127, 1)
            total = (both + both) + (across[group] + across[group + 2]) + along
            well = wells[lax.rem(number + 8, 8), group, pl.ds(8 * part, 8), :]
            value = (total - well * centre) * factor
            if stage > 1:
                older = ring[
                    stage - 2, lax.rem(number + 4, 4), own, group, pl.ds(8 + 8 * part, 8), :
                ]
                value = value - (older * last_scale() if stage == DEG else older)
            made.append(value)
        return made

    def middle_stage(stage, time):
        number = time - stage
        place = position(number)
        slot = lax.rem(number + 8, 4)
        active = time >= 2 * stage

        @pl.when(jnp.logical_and(active, place < SIDE))
        def _():
            for own in range(2):
                for part in range(3):
                    for group, value in enumerate(advance(stage, number, own, part)):
                        ring[stage, slot, own, group, pl.ds(8 + 8 * part, 8), :] = value

        @pl.when(jnp.logical_and(active, place == SIDE))
        def _():
            zero_plane(stage, slot)

    def last_stage(time):
        number = time - DEG
        place = position(number)

        @pl.when(jnp.logical_and(time >= 2 * DEG, place < SIDE))
        def _():
            plane = plane_of(place)
            for own in range(2):
                for part in range(3):
                    rows = to_rows(advance(DEG, number, own, part))
                    for j in range(3):
                        packed[pl.ds(48 * part + 2 * j + own, 8, stride=6), :] = rows[j]
            pairs = packed[...].astype(jnp.bfloat16).reshape(FLAT, 2, 128)
            staged[pl.ds(FLAT * plane, FLAT)] = pairs
            upward = 1 - downward
            low = (8 * plane + 2 * downward) // 3
            high = (8 * (plane + 1) + 2 * (1 - upward)) // 3

            def send(target, carry):
                @pl.when(target == me)
                def _():
                    pltpu.make_async_copy(
                        staged.at[pl.ds(BLOCKS * target, BLOCKS)], landed.at[:, slot_of_me], recv_sem
                    ).start()

                @pl.when(target != me)
                def _():
                    pltpu.make_async_remote_copy(
                        staged.at[pl.ds(BLOCKS * target, BLOCKS)], landed.at[:, slot_of_me],
                        send_sem, recv_sem,
                        device_id=(target // 64, lax.rem(target, 64)), device_id_type=MESH,
                    ).start()

                return carry

            lax.fori_loop(low, high, send, 0)

    def step(time, carry):
        @pl.when(time == 2 * DEG - 1)
        def _():
            pl.semaphore_wait(barrier, DEVICES - 1)
            pltpu.make_async_copy(subspace, matrix.at[:, column, depth], near_recv).start()

            def send(offset, inner):
                peer = torus_peer(orb, grid, offset * 32)
                pltpu.make_async_remote_copy(
                    subspace, matrix.at[:, column, depth], near_send, near_recv,
                    device_id=peer, device_id_type=MESH,
                ).start()
                return inner

            lax.fori_loop(1, 8, send, 0)

        @pl.when(time == 40)
        def _():
            group = matrix.at[:, column]
            pltpu.make_async_copy(group, group, near_recv).wait()

            def send(offset, inner):
                peer = torus_peer(orb, grid, offset)
                pltpu.make_async_remote_copy(
                    matrix.at[:, column], matrix.at[:, column], far_send, far_recv,
                    device_id=peer, device_id_type=MESH,
                ).start()
                return inner

            lax.fori_loop(1, 32, send, 0)

        take(time)
        for stage in range(1, DEG):
            middle_stage(stage, time)
        last_stage(time)
        return carry

    lax.fori_loop(0, STEPS, step, 0)

    near = matrix.at[:, 0, pl.ds(0, 7)]
    pltpu.make_async_copy(near, near, near_send).wait()
    far = matrix.at[:, pl.ds(0, 31)]
    pltpu.make_async_copy(far, far, far_recv).wait()
    pltpu.make_async_copy(far, far, far_send).wait()
    pltpu.make_async_copy(landed, landed, recv_sem).wait()
    sent = staged.at[pl.ds(0, BLOCKS * (DEVICES - 1))]
    pltpu.make_async_copy(sent, sent, send_sem).wait()


def sweep(orbitals, potential, subspace):
    vmem = pl.BlockSpec(memory_space=pltpu.VMEM)
    return pl.pallas_call(
        sweep_kernel,
        out_shape=(
            jax.ShapeDtypeStruct((BLOCKS, DEVICES, 2, 128), jnp.bfloat16),
            jax.ShapeDtypeStruct((4, 32, 8, 2, 128), jnp.bfloat16),
        ),
        in_specs=[vmem, vmem, vmem],
        out_specs=(vmem, vmem),
        scratch_shapes=[
            pltpu.VMEM((DEG, 4, 2, 4, 40, 128), jnp.float32),
            pltpu.VMEM((8, 4, 24, 128), jnp.float32),
            pltpu.VMEM((2 * FLAT, 128), jnp.float32),
            pltpu.VMEM((2 * FLAT, 128), jnp.float32),
            pltpu.VMEM((SIDE * FLAT, 2, 128), jnp.bfloat16),
        ] + [pltpu.SemaphoreType.DMA] * 6,
        compiler_params=pltpu.CompilerParams(
            collective_id=0, has_side_effects=True, vmem_limit_bytes=40 * 2**20
        ),
        name="sweep",
    )(orbitals, potential, subspace)


def rotate_kernel(matrix, fields, rotated):
    mixing = jnp.concatenate([matrix[i] for i in range(4)], axis=1)
    wide = jnp.concatenate([fields[i] for i in range(3)], axis=1)
    rotated[...] = lax.dot_general(
        mixing, wide, (((0,), (0,)), ((), ())), preferred_element_type=jnp.float32
    ).astype(jnp.bfloat16)


def rotate(matrix, fields):
    return pl.pallas_call(
        rotate_kernel,
        grid=(BLOCKS // 3,),
        out_shape=jax.ShapeDtypeStruct((512, BLOCKS * 128), jnp.bfloat16),
        in_specs=[
            pl.BlockSpec((4, 512, 128), lambda i: (0, 0, 0)),
            pl.BlockSpec((3, 512, 128), lambda i: (i, 0, 0)),
        ],
        out_specs=pl.BlockSpec((512, 384), lambda i: (0, i)),
        compiler_params=pltpu.CompilerParams(vmem_limit_bytes=32 * 2**20),
        name="rotate",
    )(matrix, fields)


def local(orbitals, potential, subspace):
    pairs = orbitals.reshape(2, SIDE * FLAT, 128).transpose(1, 0, 2)
    fields, matrix = sweep(
        pairs.reshape(SIDE, 2 * FLAT, 128),
        potential.reshape(SIDE, FLAT, 128),
        subspace.reshape(2, 4, 128).transpose(1, 0, 2),
    )
    return rotate(matrix.reshape(4, 512, 128), fields.reshape(BLOCKS, 512, 128))


def solution(mesh):
    placed = (P(("orb", "grid"), None), P(), P(("orb", "grid"), None))
    return jax.shard_map(
        local, mesh=mesh, in_specs=placed, out_specs=P(None, ("orb", "grid")), check_vma=False
    )
```

time: 860 us -> 172 us (0.20)
  blocking collectives: 367 us -> 0 us
  other arithmetic: 299 us -> 0 us
  local copies, waits for them, and re-layouts: 82 us -> 4.68 us
  Pallas kernels: 111 us -> 166 us
    all_gather x1 -> x0, blocking collectives: 367 us -> none  [local(): matrix = lax.all_gather(subspace, ('orb', 'grid'), axis=0, tiled=True)]
    sub x5 -> x0, other arithmetic: 155 us -> none  [advance(): (applied - centre * present) * step_table[order_index]]
    add x12 -> x0, other arithmetic: 112 us -> none  [the longest x6 109 us: hamiltonian(): edges = along_rows(cols_sum + depth_sum) + along_columns(depth_sum, GRID_N)]
    pallas_call x1, Pallas kernels: 105 us -> 160 us  [sweep(): pl.pallas_call(sweep_kernel, out_shape=(jax.ShapeDtypeStruct((BLOCKS, DEV...]
    while x30 -> x0, local copies, waits for them, and re-layouts: 48.4 us -> none
    mul x1 -> x0, other arithmetic: 28.4 us -> none  [chebyshev_filter(): (hamiltonian(fields, shaped_pot, upper_mask, lower_mask) - centre * field...]
    reshape x3 -> x0, local copies, waits for them, and re-layouts: 16.6 us -> none  [the longest x2 14.2 us: local(): result.astype(jnp.bfloat16).reshape(local_count, DEVICES, BLOCKS, 128)]
where the time goes in v2:
time: 172 us; the launch traced here: 171 us
  Pallas kernels  166 us (97%)
  local copies, waits for them, and re-layouts  4.68 us (3%)
    pallas_call x1, Pallas kernels, sweep(): pl.pallas_call(sweep_kernel, out_shape=(jax.ShapeDtypeStruct((BLOCKS, DEV...  160 us
    pallas_call x1, Pallas kernels, rotate(): pl.pallas_call(rotate_kernel, grid=(BLOCKS // 3,), out_shape=jax.ShapeDty...  6.11 us
    unnamed x6, local copies, waits for them, and re-layouts  4.68 us

profile of v2, /device:TPU:1, one launch (start us, length us, event | category | flops | bytes accessed | tf_op | source)
XLA Modules:
  0.0 170.8 jit_solution(14225146132324530038)
XLA Ops:
  0.0 0.0 copy-start
  0.0 2.0 %copy-done = bf16[2,884736]{1,0:T(2,128)(2,1)S(1)} copy-done((bf16[2,884736]{1,0:T(2,128)(2,1)S(1)}, bf16[2,884736]{1,0:T(2,128)(2,1)}, u32[]{:S(2)}) %copy-start) | copy-done | bytes 3538968
  2.0 0.0 copy-start.1
  2.0 2.0 %copy-done.1 = f32[884736]{0:T(1024)S(1)} copy-done((f32[884736]{0:T(1024)S(1)}, f32[884736]{0:T(1024)}, u32[]{:S(2)}) %copy-start.1) | copy-done | bytes 3538968
  4.0 0.0 copy-start.2
  4.0 0.7 copy-done.2
  4.7 160.0 %sweep.1 = (bf16[27,256,2,128]{3,2,1,0:T(2,128)(2,1)S(1)}, bf16[4,32,8,2,128]{4,3,2,1,0:T(2,128)(2,1)S(1)}) custom-call(bf16[96,144,128]{2,1,0:T(8,128)(2,1)S(1)} %bitcast.11, f32[96,72,128]{2,1,0:T(8,128)S(1)} %bitcast.12, bf16[4,2,128]{2,1,0:T(2,128)(2,1)S(1)} %bitcast.15), custom_call_target="tpu_custom_call" | custom-call | tf_op jit(solution)/shard_map/sweep/pallas_call | solution.py:274
  164.6 6.1 %rotate.1 = bf16[512,3456]{1,0:T(8,128)(2,1)} custom-call(bf16[4,512,128]{2,1,0:T(8,128)(2,1)S(1)} %bitcast.14, bf16[27,512,128]{2,1,0:T(8,128)(2,1)S(1)} %bitcast.13), custom_call_target="tpu_custom_call" | custom-call | tf_op jit(solution)/shard_map/rotate/pallas_call | solution.py:305
Async XLA Ops:
  0.0 2.0 %copy-start = (bf16[2,884736]{1,0:T(2,128)(2,1)S(1)}, bf16[2,884736]{1,0:T(2,128)(2,1)}, u32[]{:S(2)}) copy-start(bf16[2,884736]{1,0:T(2,128)(2,1)} %param.3) | copy-start | bytes 10616836
  2.0 2.0 %copy-start.1 = (f32[884736]{0:T(1024)S(1)}, f32[884736]{0:T(1024)}, u32[]{:S(2)}) copy-start(f32[884736]{0:T(1024)} %param.4) | copy-start | bytes 10616836
  4.0 0.7 copy-start.2

commit v3 on v2

--- a/solution.py
+++ b/solution.py
@@ -1,3 +1,5 @@
+import functools
+
 import jax
 import jax.numpy as jnp
 from jax import lax
@@ -11,7 +13,9 @@
 BLOCKS = 27
 FLAT = 72
 PERIOD = SIDE + 1
-STEPS = PERIOD + 2 * DEG
+STEPS = PERIOD + 3 * DEG + 1
+READY = 3 * DEG + 1
+GROUPS = 4
 MESH = pl.DeviceIdType.MESH
 
 TOP = 12.0
@@ -39,10 +43,11 @@
 
 
 def sweep_kernel(
-    orbitals, potential, subspace, landed, matrix,
-    ring, wells, raw, packed, staged,
-    send_sem, recv_sem, near_send, near_recv, far_send, far_recv,
+    orbitals_hbm, potential_hbm, subspace, landed, matrix,
+    orbitals, potential, ring0, ring1, ring2, ring3, ring4, ring5, wells, raw, packed, staged,
+    send_sem, recv_sem, near_send, near_recv, far_send, far_recv, orbitals_sem, potential_sem,
 ):
+    ring = (ring0, ring1, ring2, ring3, ring4, ring5)
     orb, grid = lax.axis_index("orb"), lax.axis_index("grid")
     me = orb * 64 + grid
     column = grid // 4 * 2 + lax.rem(grid, 2)
@@ -50,6 +55,12 @@
     slot_of_me = column * 8 + depth
     downward = lax.rem(grid, 2)
     barrier = pltpu.get_barrier_semaphore()
+    fetches = (
+        pltpu.make_async_copy(orbitals_hbm, orbitals, orbitals_sem),
+        pltpu.make_async_copy(potential_hbm, potential, potential_sem),
+    )
+    for fetch in fetches:
+        fetch.start()
 
     def greet(step, carry):
         peer = torus_peer(orb, grid, step)
@@ -64,13 +75,16 @@
     zeros = jnp.zeros((8, 128), jnp.float32)
 
     def clear(at, carry):
-        for own in range(2):
-            for group in range(4):
-                ring[at // 4, lax.rem(at, 4), own, group, pl.ds(0, 8), :] = zeros
-                ring[at // 4, lax.rem(at, 4), own, group, pl.ds(32, 8), :] = zeros
+        for held in ring:
+            for own in range(2):
+                for group in range(GROUPS):
+                    held[at, own, group, pl.ds(0, 8), :] = zeros
+                    held[at, own, group, pl.ds(32, 8), :] = zeros
         return carry
 
-    lax.fori_loop(0, DEG * 4, clear, 0)
+    lax.fori_loop(0, 4, clear, 0)
+    for fetch in fetches:
+        fetch.wait()
 
     own_plane = me * 3 // 8 // 3 * 3
     ordered = jnp.where(downward == 1, SIDE - 3 - own_plane, own_plane)
@@ -101,42 +115,43 @@
             jnp.where(lane < 32, middle, late),
         )
 
-    def zero_plane(stage, slot):
-        for own in range(2):
-            for group in range(4):
+    def keep(stage, slot, own, part, values):
+        rows = pl.ds(8 + 8 * part, 8)
+        for group, value in enumerate(values):
+            ring[stage][slot, own, group, rows, :] = value
+
+    def zero_plane(stage, number):
+        slot = lax.rem(number + 64, 4)
+        place = position(number)
+
+        @pl.when(place == SIDE)
+        def _():
+            for own in range(2):
                 for part in range(3):
-                    ring[stage, slot, own, group, pl.ds(8 + 8 * part, 8), :] = zeros
+                    keep(stage, slot, own, part, [zeros] * 4)
 
     def take(time):
         place = position(time)
         slot = lax.rem(time, 4)
-        well = lax.rem(time, 8)
-
-        @pl.when(place < SIDE)
-        def _():
-            plane = plane_of(place)
-            raw[...] = orbitals[plane].astype(jnp.float32)
-            for part in range(3):
-                rows = [potential[plane, pl.ds(24 * part + j, 8, stride=3), :] for j in range(3)]
-                for group, line in enumerate(to_lines(rows)):
-                    wells[well, group, pl.ds(8 * part, 8), :] = 3.0 * line + 6.0
-                for own in range(2):
-                    rows = [raw[pl.ds(48 * part + 2 * j + own, 8, stride=6), :] for j in range(3)]
-                    for group, line in enumerate(to_lines(rows)):
-                        ring[0, slot, own, group, pl.ds(8 + 8 * part, 8), :] = line
-
-        @pl.when(place == SIDE)
-        def _():
-            zero_plane(0, slot)
+        well = lax.rem(time, 16)
+        plane = plane_of(jnp.minimum(place, SIDE - 1))
+        raw[...] = orbitals[plane].astype(jnp.float32)
+        for part in range(3):
+            rows = [potential[plane, pl.ds(24 * part + j, 8, stride=3), :] for j in range(3)]
+            for group, line in enumerate(to_lines(rows)):
+                wells[well, group, pl.ds(8 * part, 8), :] = 3.0 * line + 6.0
+            for own in range(2):
+                rows = [raw[pl.ds(48 * part + 2 * j + own, 8, stride=6), :] for j in range(3)]
+                keep(0, slot, own, part, to_lines(rows))
 
     def advance(stage, number, own, part):
         def read(plane):
-            at = lax.rem(plane + 4, 4)
+            at = lax.rem(plane + 64, 4)
             rows = [
-                ring[stage - 1, at, own, group, pl.ds(8 + 8 * part, 8), :] for group in range(4)
+                ring[stage - 1][at, own, group, pl.ds(8 + 8 * part, 8), :] for group in range(4)
             ]
-            before = ring[stage - 1, at, own, 3, pl.ds(7 + 8 * part, 8), :]
-            after = ring[stage - 1, at, own, 0, pl.ds(9 + 8 * part, 8), :]
+            before = ring[stage - 1][at, own, 3, pl.ds(7 + 8 * part, 8), :]
+            after = ring[stage - 1][at, own, 0, pl.ds(9 + 8 * part, 8), :]
             return [before] + rows + [after]
 
         behind, here, ahead = read(number - 1), read(number), read(number + 1)
@@ -156,50 +171,26 @@
             wide = both + (centre + centre)
             along = pltpu.roll(wide, 1, 1) + pltpu.roll(wide, 127, 1)
             total = (both + both) + (across[group] + across[group + 2]) + along
-            well = wells[lax.rem(number + 8, 8), group, pl.ds(8 * part, 8), :]
+            well = wells[lax.rem(number + 64, 16), group, pl.ds(8 * part, 8), :]
             value = (total - well * centre) * factor
             if stage > 1:
-                older = ring[
-                    stage - 2, lax.rem(number + 4, 4), own, group, pl.ds(8 + 8 * part, 8), :
+                older = ring[stage - 2][
+                    lax.rem(number + 64, 4), own, group, pl.ds(8 + 8 * part, 8), :
                 ]
                 value = value - (older * last_scale() if stage == DEG else older)
             made.append(value)
         return made
 
-    def middle_stage(stage, time):
-        number = time - stage
-        place = position(number)
-        slot = lax.rem(number + 8, 4)
-        active = time >= 2 * stage
-
-        @pl.when(jnp.logical_and(active, place < SIDE))
-        def _():
-            for own in range(2):
-                for part in range(3):
-                    for group, value in enumerate(advance(stage, number, own, part)):
-                        ring[stage, slot, own, group, pl.ds(8 + 8 * part, 8), :] = value
-
-        @pl.when(jnp.logical_and(active, place == SIDE))
-        def _():
-            zero_plane(stage, slot)
-
-    def last_stage(time):
-        number = time - DEG
-        place = position(number)
-
-        @pl.when(jnp.logical_and(time >= 2 * DEG, place < SIDE))
+    def pack(time):
+        place = position(time - 2 * DEG - 1)
+
+        @pl.when(jnp.logical_and(time >= READY, place < SIDE))
         def _():
             plane = plane_of(place)
-            for own in range(2):
-                for part in range(3):
-                    rows = to_rows(advance(DEG, number, own, part))
-                    for j in range(3):
-                        packed[pl.ds(48 * part + 2 * j + own, 8, stride=6), :] = rows[j]
             pairs = packed[...].astype(jnp.bfloat16).reshape(FLAT, 2, 128)
             staged[pl.ds(FLAT * plane, FLAT)] = pairs
-            upward = 1 - downward
             low = (8 * plane + 2 * downward) // 3
-            high = (8 * (plane + 1) + 2 * (1 - upward)) // 3
+            high = (8 * (plane + 1) + 2 * downward) // 3
 
             def send(target, carry):
                 @pl.when(target == me)
@@ -220,8 +211,23 @@
 
             lax.fori_loop(low, high, send, 0)
 
+    def stages(deepest, time):
+        for stage in range(deepest, 0, -1):
+            number = time - 2 * stage
+            slot = lax.rem(number + 64, 4)
+            for own in range(2):
+                for part in range(3):
+                    keep(stage, slot, own, part, advance(stage, number, own, part))
+        take(time)
+        for stage in range(deepest + 1):
+            zero_plane(stage, time - 2 * stage)
+
+    def warm(deepest, time, carry):
+        stages(deepest, time)
+        return carry
+
     def step(time, carry):
-        @pl.when(time == 2 * DEG - 1)
+        @pl.when(time == READY - 1)
         def _():
             pl.semaphore_wait(barrier, DEVICES - 1)
             pltpu.make_async_copy(subspace, matrix.at[:, column, depth], near_recv).start()
@@ -236,7 +242,7 @@
 
             lax.fori_loop(1, 8, send, 0)
 
-        @pl.when(time == 40)
+        @pl.when(time == 50)
         def _():
             group = matrix.at[:, column]
             pltpu.make_async_copy(group, group, near_recv).wait()
@@ -251,13 +257,19 @@
 
             lax.fori_loop(1, 32, send, 0)
 
-        take(time)
-        for stage in range(1, DEG):
-            middle_stage(stage, time)
-        last_stage(time)
+        pack(time)
+        for own in range(2):
+            for part in range(3):
+                rows = to_rows(advance(DEG, time - 2 * DEG, own, part))
+                for j in range(3):
+                    packed[pl.ds(48 * part + 2 * j + own, 8, stride=6), :] = rows[j]
+        stages(DEG - 1, time)
         return carry
 
-    lax.fori_loop(0, STEPS, step, 0)
+    for deepest in (1, 3, 5):
+        start = 3 * deepest - 3
+        lax.fori_loop(start, start + 6, functools.partial(warm, deepest), 0)
+    lax.fori_loop(3 * DEG, STEPS, step, 0)
 
     near = matrix.at[:, 0, pl.ds(0, 7)]
     pltpu.make_async_copy(near, near, near_send).wait()
@@ -271,21 +283,24 @@
 
 def sweep(orbitals, potential, subspace):
     vmem = pl.BlockSpec(memory_space=pltpu.VMEM)
+    hbm = pl.BlockSpec(memory_space=pltpu.HBM)
     return pl.pallas_call(
         sweep_kernel,
         out_shape=(
             jax.ShapeDtypeStruct((BLOCKS, DEVICES, 2, 128), jnp.bfloat16),
             jax.ShapeDtypeStruct((4, 32, 8, 2, 128), jnp.bfloat16),
         ),
-        in_specs=[vmem, vmem, vmem],
+        in_specs=[hbm, hbm, vmem],
         out_specs=(vmem, vmem),
         scratch_shapes=[
-            pltpu.VMEM((DEG, 4, 2, 4, 40, 128), jnp.float32),
-            pltpu.VMEM((8, 4, 24, 128), jnp.float32),
+            pltpu.VMEM((SIDE, 2 * FLAT, 128), jnp.bfloat16),
+            pltpu.VMEM((SIDE, FLAT, 128), jnp.float32),
+        ] + [pltpu.VMEM((4, 2, GROUPS, 40, 128), jnp.float32)] * DEG + [
+            pltpu.VMEM((16, 4, 24, 128), jnp.float32),
             pltpu.VMEM((2 * FLAT, 128), jnp.float32),
             pltpu.VMEM((2 * FLAT, 128), jnp.float32),
             pltpu.VMEM((SIDE * FLAT, 2, 128), jnp.bfloat16),
-        ] + [pltpu.SemaphoreType.DMA] * 6,
+        ] + [pltpu.SemaphoreType.DMA] * 8,
         compiler_params=pltpu.CompilerParams(
             collective_id=0, has_side_effects=True, vmem_limit_bytes=40 * 2**20
         ),

time: 172 us -> 123 us (0.72)
  the two profiles are of different devices: /device:TPU:1 before, /device:TPU:73 now
where the time goes in v3:
time: 123 us
  Pallas kernels  118 us (96%)
  local copies, waits for them, and re-layouts  4.68 us (4%)
    pallas_call x1, Pallas kernels, sweep(): pl.pallas_call(sweep_kernel, out_shape=(jax.ShapeDtypeStruct((BLOCKS, DEV...  112 us
    pallas_call x1, Pallas kernels, rotate(): pl.pallas_call(rotate_kernel, grid=(BLOCKS // 3,), out_shape=jax.ShapeDty...  6.1 us
    unnamed x6, local copies, waits for them, and re-layouts  4.68 us

profile of v3, /device:TPU:73, one launch (start us, length us, event | category | flops | bytes accessed | tf_op | source)
XLA Modules:
  0.0 122.5 jit_solution(8858299324040343411)
XLA Ops:
  0.0 0.0 copy-start
  0.0 2.0 %copy-done = bf16[2,884736]{1,0:T(2,128)(2,1)S(1)} copy-done((bf16[2,884736]{1,0:T(2,128)(2,1)S(1)}, bf16[2,884736]{1,0:T(2,128)(2,1)}, u32[]{:S(2)}) %copy-start) | copy-done | bytes 3538968
  2.0 0.0 copy-start.1
  2.0 2.0 %copy-done.1 = f32[884736]{0:T(1024)S(1)} copy-done((f32[884736]{0:T(1024)S(1)}, f32[884736]{0:T(1024)}, u32[]{:S(2)}) %copy-start.1) | copy-done | bytes 3538968
  4.0 0.0 copy-start.2
  4.0 0.7 copy-done.2
  4.7 111.7 %sweep.1 = (bf16[27,256,2,128]{3,2,1,0:T(2,128)(2,1)S(1)}, bf16[4,32,8,2,128]{4,3,2,1,0:T(2,128)(2,1)S(1)}) custom-call(bf16[96,144,128]{2,1,0:T(8,128)(2,1)S(1)} %bitcast.11, f32[96,72,128]{2,1,0:T(8,128)S(1)} %bitcast.12, bf16[4,2,128]{2,1,0:T(2,128)(2,1)S(1)} %bitcast.15), custom_call_target="tpu_custom_call" | custom-call | tf_op jit(solution)/shard_map/sweep/pallas_call | solution.py:287
  116.4 6.1 %rotate.1 = bf16[512,3456]{1,0:T(8,128)(2,1)} custom-call(bf16[4,512,128]{2,1,0:T(8,128)(2,1)S(1)} %bitcast.14, bf16[27,512,128]{2,1,0:T(8,128)(2,1)S(1)} %bitcast.13), custom_call_target="tpu_custom_call" | custom-call | tf_op jit(solution)/shard_map/rotate/pallas_call | solution.py:320
Async XLA Ops:
  0.0 2.0 %copy-start = (bf16[2,884736]{1,0:T(2,128)(2,1)S(1)}, bf16[2,884736]{1,0:T(2,128)(2,1)}, u32[]{:S(2)}) copy-start(bf16[2,884736]{1,0:T(2,128)(2,1)} %param.3) | copy-start | bytes 10616836
  2.0 2.0 %copy-start.1 = (f32[884736]{0:T(1024)S(1)}, f32[884736]{0:T(1024)}, u32[]{:S(2)}) copy-start(f32[884736]{0:T(1024)} %param.4) | copy-start | bytes 10616836
  4.0 0.7 copy-start.2

commit v4 on v3

--- a/solution.py
+++ b/solution.py
@@ -46,6 +46,7 @@
     orbitals_hbm, potential_hbm, subspace, landed, matrix,
     orbitals, potential, ring0, ring1, ring2, ring3, ring4, ring5, wells, raw, packed, staged,
     send_sem, recv_sem, near_send, near_recv, far_send, far_recv, orbitals_sem, potential_sem,
+    column_sem,
 ):
     ring = (ring0, ring1, ring2, ring3, ring4, ring5)
     orb, grid = lax.axis_index("orb"), lax.axis_index("grid")
@@ -67,7 +68,8 @@
         pl.semaphore_signal(barrier, inc=1, device_id=peer, device_id_type=MESH)
         return carry
 
-    lax.fori_loop(1, DEVICES, greet, 0)
+    lax.fori_loop(1, 32, greet, 0)
+    lax.fori_loop(1, 8, lambda step, carry: greet(32 * step, carry), 0)
 
     lane = lax.broadcasted_iota(jnp.int32, (8, 128), 1)
     inside = lane < SIDE
@@ -85,10 +87,21 @@
     lax.fori_loop(0, 4, clear, 0)
     for fetch in fetches:
         fetch.wait()
+    pl.semaphore_wait(barrier, 38)
+
+    def confirm(step, carry):
+        peer = torus_peer(orb, grid, step)
+        pl.semaphore_signal(column_sem, inc=1, device_id=peer, device_id_type=MESH)
+        return carry
+
+    lax.fori_loop(1, 32, confirm, 0)
 
     own_plane = me * 3 // 8 // 3 * 3
     ordered = jnp.where(downward == 1, SIDE - 3 - own_plane, own_plane)
-    base = lax.rem(ordered + 24, SIDE) - DEG + PERIOD
+    near_half = lax.rem(grid // 2, 2)
+    quarters = jnp.where(downward == 1, 2 - 2 * near_half, 1 + 2 * near_half)
+    shift = 24 * quarters + 12 * lax.rem(grid // 4, 2)
+    base = lax.rem(ordered + shift, SIDE) - DEG + PERIOD
 
     def position(number):
         return lax.rem(base + number, PERIOD)
@@ -229,7 +242,7 @@
     def step(time, carry):
         @pl.when(time == READY - 1)
         def _():
-            pl.semaphore_wait(barrier, DEVICES - 1)
+            pl.semaphore_wait(column_sem, 31)
             pltpu.make_async_copy(subspace, matrix.at[:, column, depth], near_recv).start()
 
             def send(offset, inner):
@@ -300,19 +313,23 @@
             pltpu.VMEM((2 * FLAT, 128), jnp.float32),
             pltpu.VMEM((2 * FLAT, 128), jnp.float32),
             pltpu.VMEM((SIDE * FLAT, 2, 128), jnp.bfloat16),
-        ] + [pltpu.SemaphoreType.DMA] * 8,
+        ] + [pltpu.SemaphoreType.DMA] * 8 + [pltpu.SemaphoreType.REGULAR],
         compiler_params=pltpu.CompilerParams(
-            collective_id=0, has_side_effects=True, vmem_limit_bytes=40 * 2**20
+            collective_id=0, has_side_effects=True, vmem_limit_bytes=56 * 2**20
         ),
         name="sweep",
     )(orbitals, potential, subspace)
 
 
-def rotate_kernel(matrix, fields, rotated):
-    mixing = jnp.concatenate([matrix[i] for i in range(4)], axis=1)
+def rotate_kernel(matrix, fields, rotated, turned):
+    @pl.when(pl.program_id(0) == 0)
+    def _():
+        for i in range(4):
+            turned[pl.ds(128 * i, 128), :] = matrix[i].T
+
     wide = jnp.concatenate([fields[i] for i in range(3)], axis=1)
-    rotated[...] = lax.dot_general(
-        mixing, wide, (((0,), (0,)), ((), ())), preferred_element_type=jnp.float32
+    rotated[...] = jnp.dot(
+        turned[...], wide, preferred_element_type=jnp.float32
     ).astype(jnp.bfloat16)
 
 
@@ -326,7 +343,8 @@
             pl.BlockSpec((3, 512, 128), lambda i: (i, 0, 0)),
         ],
         out_specs=pl.BlockSpec((512, 384), lambda i: (0, i)),
-        compiler_params=pltpu.CompilerParams(vmem_limit_bytes=32 * 2**20),
+        scratch_shapes=[pltpu.VMEM((512, 512), jnp.bfloat16)],
+        compiler_params=pltpu.CompilerParams(vmem_limit_bytes=58 * 2**20),
         name="rotate",
     )(matrix, fields)
 

time: 123 us -> 116 us (0.943)
  the two profiles are of different devices: /device:TPU:73 before, /device:TPU:1 now
where the time goes in v4:
time: 116 us; the launch traced here: 115 us
  Pallas kernels  115 us (99%)
    pallas_call x1, Pallas kernels, sweep(): pl.pallas_call(sweep_kernel, out_shape=(jax.ShapeDtypeStruct((BLOCKS, DEV...  106 us
    pallas_call x1, Pallas kernels, rotate(): pl.pallas_call(rotate_kernel, grid=(BLOCKS // 3,), out_shape=jax.ShapeDty...  9 us

profile of v4, /device:TPU:1, one launch (start us, length us, event | category | flops | bytes accessed | tf_op | source)
XLA Modules:
  0.0 115.4 jit_solution(18299740844458186493)
XLA Ops:
  0.0 106.4 %sweep.1 = (bf16[27,256,2,128]{3,2,1,0:T(2,128)(2,1)}, bf16[4,32,8,2,128]{4,3,2,1,0:T(2,128)(2,1)}) custom-call(bf16[96,144,128]{2,1,0:T(8,128)(2,1)} %bitcast.11, f32[96,72,128]{2,1,0:T(8,128)} %bitcast.12, bf16[4,2,128]{2,1,0:T(2,128)(2,1)} %bitcast.15), custom_call_target="tpu_custom_call" | custom-call | tf_op jit(solution)/shard_map/sweep/pallas_call | solution.py:300
  106.4 9.0 %rotate.1 = bf16[512,3456]{1,0:T(8,128)(2,1)} custom-call(bf16[4,512,128]{2,1,0:T(8,128)(2,1)} %bitcast.14, bf16[27,512,128]{2,1,0:T(8,128)(2,1)} %bitcast.13), custom_call_target="tpu_custom_call" | custom-call | tf_op jit(solution)/shard_map/rotate/pallas_call | solution.py:337

commit v5 on v4

--- a/solution.py
+++ b/solution.py
@@ -327,7 +327,7 @@
         for i in range(4):
             turned[pl.ds(128 * i, 128), :] = matrix[i].T
 
-    wide = jnp.concatenate([fields[i] for i in range(3)], axis=1)
+    wide = jnp.concatenate([fields[i] for i in range(9)], axis=1)
     rotated[...] = jnp.dot(
         turned[...], wide, preferred_element_type=jnp.float32
     ).astype(jnp.bfloat16)
@@ -336,13 +336,13 @@
 def rotate(matrix, fields):
     return pl.pallas_call(
         rotate_kernel,
-        grid=(BLOCKS // 3,),
+        grid=(BLOCKS // 9,),
         out_shape=jax.ShapeDtypeStruct((512, BLOCKS * 128), jnp.bfloat16),
         in_specs=[
             pl.BlockSpec((4, 512, 128), lambda i: (0, 0, 0)),
-            pl.BlockSpec((3, 512, 128), lambda i: (i, 0, 0)),
+            pl.BlockSpec((9, 512, 128), lambda i: (i, 0, 0)),
         ],
-        out_specs=pl.BlockSpec((512, 384), lambda i: (0, i)),
+        out_specs=pl.BlockSpec((512, 1152), lambda i: (0, i)),
         scratch_shapes=[pltpu.VMEM((512, 512), jnp.bfloat16)],
         compiler_params=pltpu.CompilerParams(vmem_limit_bytes=58 * 2**20),
         name="rotate",

time: 116 us -> 113 us (0.974)
  Pallas kernels: 115 us -> 112 us
    pallas_call x1, Pallas kernels: 9 us -> 6.01 us  [rotate(): pl.pallas_call(rotate_kernel, grid=(BLOCKS // 9,), out_shape=jax.ShapeDty...]
where the time goes in v5:
time: 113 us; the launch traced here: 112 us
  Pallas kernels  112 us (99%)
    pallas_call x1, Pallas kernels, sweep(): pl.pallas_call(sweep_kernel, out_shape=(jax.ShapeDtypeStruct((BLOCKS, DEV...  106 us
    pallas_call x1, Pallas kernels, rotate(): pl.pallas_call(rotate_kernel, grid=(BLOCKS // 9,), out_shape=jax.ShapeDty...  6.01 us

profile of v5, /device:TPU:1, one launch (start us, length us, event | category | flops | bytes accessed | tf_op | source)
XLA Modules:
  0.0 112.4 jit_solution(9228537363320299777)
XLA Ops:
  0.0 106.4 %sweep.1 = (bf16[27,256,2,128]{3,2,1,0:T(2,128)(2,1)}, bf16[4,32,8,2,128]{4,3,2,1,0:T(2,128)(2,1)}) custom-call(bf16[96,144,128]{2,1,0:T(8,128)(2,1)} %bitcast.11, f32[96,72,128]{2,1,0:T(8,128)} %bitcast.12, bf16[4,2,128]{2,1,0:T(2,128)(2,1)} %bitcast.15), custom_call_target="tpu_custom_call" | custom-call | tf_op jit(solution)/shard_map/sweep/pallas_call | solution.py:300
  106.4 6.0 %rotate.1 = bf16[512,3456]{1,0:T(8,128)(2,1)} custom-call(bf16[4,512,128]{2,1,0:T(8,128)(2,1)} %bitcast.14, bf16[27,512,128]{2,1,0:T(8,128)(2,1)} %bitcast.13), custom_call_target="tpu_custom_call" | custom-call | tf_op jit(solution)/shard_map/rotate/pallas_call | solution.py:337
